TPU v7x, 32 devices: a whole 2x2x4 slice. The times are simulated.
32 devices in a mesh: wide: 8 (over y, x, core), narrow: 4 (over z).
Axes of the slice: x: 2, y: 2, z: 4, core: 2. Of those that a mesh axis runs over, the one named last changes fastest.
Arguments:
- hidden: bfloat16 [96, 512, 768], P(('wide', 'narrow')), may hold values from -6 to 6
- lengths: int32 [96], P(('wide', 'narrow')), may hold values from 16 to 512, as said below
- slot_order: int32 [96], P(('wide', 'narrow')), may hold values from 0 to 2, as said below
- labels: int32 [96], P(('wide', 'narrow')), may hold values from -1 to 2, as said below
- w_qkv: bfloat16 [2, 768, 2304], replicated, may hold values from -0.21875 to 0.21875
- b_query: float32 [2, 768], replicated, may hold values from -3 to 3
- b_value: float32 [2, 768], replicated, may hold values from -3 to 3
- w_out: bfloat16 [2, 768, 768], replicated, may hold values from -0.625 to 0.625
- b_out: float32 [2, 768], replicated, may hold values from -3 to 3
- ln1_gain: float32 [2, 768], replicated, may hold values from 0.1 to 1.9
- ln1_bias: float32 [2, 768], replicated, may hold values from -3 to 3
- w_in: bfloat16 [2, 768, 3072], replicated, may hold values from -0.21875 to 0.21875
- b_in: float32 [2, 3072], replicated, may hold values from -3 to 3
- w_back: bfloat16 [2, 3072, 768], replicated, may hold values from -0.15625 to 0.15625
- b_back: float32 [2, 768], replicated, may hold values from -3 to 3
- ln2_gain: float32 [2, 768], replicated, may hold values from 0.1 to 1.9
- ln2_bias: float32 [2, 768], replicated, may hold values from -3 to 3
- pool_w: float32 [2, 768, 768], replicated, may hold values from -0.21875 to 0.21875
- pool_b: float32 [2, 768], replicated, may hold values from -3 to 3
- cls_w: float32 [2, 768, 3], replicated, may hold values from -0.625 to 0.625
- cls_b: float32 [2, 3], replicated, may hold values from -3 to 3
Outputs:
- block_states: bfloat16 [2, 96, 512, 768], P(None, ('wide', 'narrow'))
- logits: float32 [2, 96, 3], P(None, ('wide', 'narrow'))
- losses: float32 [2], replicated
- grad_pool_w: float32 [2, 768, 768], replicated
- grad_pool_b: float32 [2, 768], replicated
- grad_cls_w: float32 [2, 768, 3], replicated
- grad_cls_b: float32 [2, 3], replicated
- first_grads: float32 [2, 96, 768], P(None, ('wide', 'narrow'))
Inputs may be any that keep to these rules, and one draw needn't show every extreme that they name: `lengths`: sequence 0 has length 512; the last sequence has length 16. `slot_order`: within each device's 3 slots every local index appears once. `labels`: the first arriving sequence of each device carries a label.
All inputs are finite; a program needn't handle non-finite values.
Results may differ from a plain program's by a relative error of at most 0.0085.
Values sent between devices are 32-bit elements; how exact they have to be, the bound alone decides.
A program may use at most 256 MiB of HBM per device.

v0:
```python
import math

import jax
import jax.numpy as jnp
from jax import lax
from jax.sharding import PartitionSpec as P

HEADS = 12
HEAD = 64


PRECISE = lax.Precision.HIGHEST
epsilon = 1e-12


def layer_norm(values, gain, shift):
    center = values - jnp.mean(values, -1, keepdims=True)
    spread = jnp.mean(center * center, -1, keepdims=True)
    return center * lax.rsqrt(spread + epsilon) * gain + shift


def block_forward(states, seq_lengths, weights):
    (
        w_qkv,
        b_query,
        b_value,
        w_out,
        b_out,
        ln1_gain,
        ln1_bias,
        w_in,
        b_in,
        w_back,
        b_back,
        ln2_gain,
        ln2_bias,
    ) = weights
    groups, length, width = states.shape
    bf16 = jnp.bfloat16
    f32 = jnp.float32
    rows = states.reshape(groups * length, width)
    joined = jnp.dot(rows, w_qkv, preferred_element_type=f32)
    queries = (joined[:, :width] + b_query).astype(bf16).reshape(groups, length, HEADS, HEAD)
    keys_low = joined[:, width : 2 * width].astype(bf16).reshape(groups, length, HEADS, HEAD)
    values_low = (
        (joined[:, 2 * width :] + b_value).astype(bf16).reshape(groups, length, HEADS, HEAD)
    )
    scores = jnp.einsum(
        "gqhd,gkhd->ghqk", queries, keys_low, preferred_element_type=f32
    ) * HEAD ** (-0.5)
    visible = jnp.arange(length, dtype=jnp.int32)[None, :] < seq_lengths[:, None]
    scores = jnp.where(visible[:, None, None, :], scores, -1e30)
    highest = jnp.max(scores, -1, keepdims=True)
    raised = jnp.exp(scores - highest)
    probs = (raised / jnp.sum(raised, -1, keepdims=True)).astype(bf16)
    context = jnp.einsum("ghqk,gkhd->gqhd", probs, values_low, preferred_element_type=f32).astype(
        bf16
    )
    context = context.reshape(groups * length, width)
    attended = jnp.dot(context, w_out, preferred_element_type=f32) + b_out
    middle = layer_norm(rows.astype(f32) + attended, ln1_gain, ln1_bias)
    expanded = jax.nn.gelu(
        jnp.dot(middle.astype(bf16), w_in, preferred_element_type=f32) + b_in, approximate=False
    ).astype(bf16)
    result = layer_norm(
        middle + jnp.dot(expanded, w_back, preferred_element_type=f32) + b_back, ln2_gain, ln2_bias
    )
    return result.astype(bf16).reshape(groups, length, width)


def ramp_terms(first_states, label_values, pool_weight, pool_bias, cls_weight, cls_bias):
    f32 = jnp.float32
    pooled = jnp.tanh(jnp.dot(first_states, pool_weight, precision=PRECISE) + pool_bias)
    scores = jnp.dot(pooled, cls_weight, precision=PRECISE) + cls_bias
    highest = jnp.max(scores, -1, keepdims=True)
    raised = jnp.exp(scores - highest)
    totals = jnp.sum(raised, -1, keepdims=True)
    log_total = highest[:, 0] + jnp.log(totals[:, 0])
    classes_row = jnp.arange(cls_weight.shape[1], dtype=f32)[None, :]
    onehot = (label_values[:, None] == classes_row).astype(f32)
    labelled = (label_values >= 0).astype(f32)
    loss_sum = jnp.sum(labelled * (log_total - jnp.sum(scores * onehot, -1)))
    grad_scores = labelled[:, None] * (raised / totals - onehot)
    grad_cls_weight = jnp.dot(pooled.T, grad_scores, precision=PRECISE)
    grad_cls_bias = jnp.sum(grad_scores, 0)
    grad_inner = jnp.dot(grad_scores, cls_weight.T, precision=PRECISE) * (1.0 - pooled * pooled)
    grad_pool_weight = jnp.dot(first_states.T, grad_inner, precision=PRECISE)
    grad_pool_bias = jnp.sum(grad_inner, 0)
    grad_first = jnp.dot(grad_inner, pool_weight.T, precision=PRECISE)
    return (
        scores,
        loss_sum,
        (grad_pool_weight, grad_pool_bias, grad_cls_weight, grad_cls_bias),
        grad_first,
    )


def local(
    hidden,
    lengths,
    slot_order,
    labels,
    w_qkv,
    b_query,
    b_value,
    w_out,
    b_out,
    ln1_gain,
    ln1_bias,
    w_in,
    b_in,
    w_back,
    b_back,
    ln2_gain,
    ln2_bias,
    pool_w,
    pool_b,
    cls_w,
    cls_b,
):
    f32 = jnp.float32
    states = jnp.take(hidden, slot_order, axis=0)
    seq_lengths = jnp.take(lengths, slot_order, axis=0)
    label_values = jnp.take(labels, slot_order, axis=0).astype(f32)
    depth = w_qkv.shape[0]
    stacks = (
        w_qkv,
        b_query,
        b_value,
        w_out,
        b_out,
        ln1_gain,
        ln1_bias,
        w_in,
        b_in,
        w_back,
        b_back,
        ln2_gain,
        ln2_bias,
    )
    outputs_all = []
    for number in range(depth):
        weights = tuple((stacked[number] for stacked in stacks))
        states = block_forward(states, seq_lengths, weights)
        outputs_all.append(states)
    firsts = [kept[:, 0, :].astype(f32) for kept in outputs_all]
    logit_list = []
    loss_list = []
    grad_lists = ([], [], [], [])
    first_list = []
    pieces = []
    shapes = []
    locals_first = []
    loss_sums = []
    for number in range(depth):
        scores, loss_sum, grads, grad_first = ramp_terms(
            firsts[number],
            label_values,
            pool_w[number],
            pool_b[number],
            cls_w[number],
            cls_b[number],
        )
        logit_list.append(scores)
        locals_first.append(grad_first)
        loss_sums.append(loss_sum)
        for member in grads:
            pieces.append(member.reshape(-1))
            shapes.append(member.shape)
    pieces.append(jnp.stack(loss_sums))
    pieces.append(jnp.sum((label_values >= 0).astype(f32)).reshape(1))
    bucket = jnp.concatenate(pieces)
    devices = lax.axis_size(("wide", "narrow"))
    length_used = bucket.shape[0]
    padded_length = -(-length_used // devices) * devices
    bucket = jnp.pad(bucket, (0, padded_length - length_used))
    share = lax.psum_scatter(bucket, ("wide", "narrow"), scatter_dimension=0, tiled=True)
    summed = lax.all_gather(share, ("wide", "narrow"), axis=0, tiled=True)
    offset = 0
    unpacked = []
    for shape in shapes:
        amount = math.prod(shape)
        unpacked.append(summed[offset : offset + amount].reshape(shape))
        offset += amount
    totals_loss = summed[offset : offset + depth]
    count = summed[offset + depth]
    for number in range(depth):
        for slot_number in range(4):
            grad_lists[slot_number].append(unpacked[4 * number + slot_number] / count)
        loss_list.append(totals_loss[number] / count)
        first_list.append(locals_first[number] / count)
    block_states = jnp.stack(outputs_all)
    return (
        block_states,
        jnp.stack(logit_list),
        jnp.stack(loss_list),
        jnp.stack(grad_lists[0]),
        jnp.stack(grad_lists[1]),
        jnp.stack(grad_lists[2]),
        jnp.stack(grad_lists[3]),
        jnp.stack(first_list),
    )


def solution(mesh):
    return jax.shard_map(
        local,
        mesh=mesh,
        in_specs=(
            P(("wide", "narrow"), None, None),
            P(("wide", "narrow")),
            P(("wide", "narrow")),
            P(("wide", "narrow")),
            P(),
            P(),
            P(),
            P(),
            P(),
            P(),
            P(),
            P(),
            P(),
            P(),
            P(),
            P(),
            P(),
            P(),
            P(),
            P(),
            P(),
        ),
        out_specs=(
            P(None, ("wide", "narrow"), None, None),
            P(None, ("wide", "narrow"), None),
            P(),
            P(),
            P(),
            P(),
            P(),
            P(None, ("wide", "narrow"), None),
        ),
        check_vma=False,
    )
```

profile of v0, /device:TPU:0, one launch (start us, length us, event | category | flops | bytes accessed | tf_op | source)
XLA Modules:
  0.0 818.1 jit_solution(6932704177683243392)
XLA Ops:
  7.2 1.5 slice_reduce_fusion.7
  8.7 0.7 compare_select_fusion
  9.4 2.2 gather_fusion
  11.5 1.3 gather_fusion.2
  12.8 1.2 fusion.216
  14.0 2.0 broadcast_select_fusion
  16.0 8.0 fusion.136
  23.9 5.0 copy-done.4
  29.2 6.6 reshape.281
  36.4 6.7 fusion.99
  43.2 8.2 %reshape.280 = bf16[3,512,12,64]{3,2,1,0:T(8,128)(2,1)} reshape(bf16[1536,768]{1,0:T(8,128)(2,1)} %get-tuple-element.70) | data formatting | bytes 4718592 | tf_op jit(solution)/shard_map/reshape | solution.py:43
  52.1 8.2 %reshape.279 = bf16[3,512,12,64]{3,2,1,0:T(8,128)(2,1)} reshape(bf16[1536,768]{1,0:T(8,128)(2,1)} %get-tuple-element.69) | data formatting | bytes 4718592 | tf_op jit(solution)/shard_map/reshape | solution.py:46
  60.3 21.0 %fusion.110 = f32[3,12,512,512]{2,3,1,0:T(8,128)} fusion(bf16[3,512,12,64]{3,2,1,0:T(8,128)(2,1)} %reshape.281, bf16[3,512,12,64]{3,2,1,0:T(8,128)(2,1)} %reshape.280), kind=kOutput, calls=%fused_computation.143 | convolution fusion | flops 1207959552 | bytes 42467328 | tf_op jit(solution)/shard_map/gqhd,gkhd->ghqk/dot_general | solution.py:48
  81.3 39.8 %fusion.289 = (f32[3,12,512]{2,1,0:T(8,128)S(1)}, f32[3,12,512,512]{2,3,1,0:T(8,128)}) fusion(f32[3,12,512,512]{2,3,1,0:T(8,128)} %fusion.110, pred[3,512]{1,0:T(4,128)(4,1)S(1)} %iota_compare_fusion), kind=kOutput, calls=%fused_computation.359 | output fusion | flops 56623616 | bytes 75572736 | tf_op jit(solution)/shard_map/sub | solution.py:54
  121.1 16.3 %convert_bitcast_fusion.1 = bf16[3,512,12,64]{1,3,2,0:T(8,128)(2,1)S(1)} fusion(f32[3,12,512,512]{2,3,1,0:T(8,128)} %get-tuple-element.91, f32[3,12,512]{2,1,0:T(8,128)S(1)} %get-tuple-element.90, bf16[3,512,12,64]{3,2,1,0:T(8,128)(2,1)} %reshape.279), kind=kOutput, calls=%fused_computation.191 | convolution fusion | flops 1228013568 | bytes 42541056 | tf_op jit(solution)/shard_map/ghqk,gkhd->gqhd/dot_general | solution.py:56
  137.4 2.0 copy.73
  139.4 2.2 copy.112
  142.8 4.5 fusion.290
  149.2 52.3 %fusion.6.clone.3.clone.5 = bf16[1536,3072]{1,0:T(8,128)(2,1)} fusion(f32[3072]{0:T(1024)S(1)} %bitcast.187, bf16[2,768,3072]{2,1,0:T(8,128)(2,1)} %param.34, f32[1536,768]{1,0:T(8,128)S(1)} %get-tuple-element.93, f32[768]{0:T(1024)S(1)} %get-tuple-element.112, f32[768]{0:T(1024)S(1)} %get-tuple-element.40, ...), kind=kOutput, calls=%fused_computation.17.clone.clone.clone.clone.clone.clone.clone.2 | convolution fusion | flops 7565082624 | bytes 18905088 | tf_op jit(solution)/shard_map/dot_general | solution.py:63
  201.6 10.7 %fusion.291 = (f32[1536]{0:T(1024)S(1)}, f32[1536,768]{1,0:T(8,128)S(1)}) fusion(f32[768]{0:T(1024)S(1)} %get-tuple-element.44, bf16[2,3072,768]{2,1,0:T(8,128)(2,1)S(1)} %bitcast.193, f32[1536,768]{1,0:T(8,128)S(1)} %get-tuple-element.93, f32[768]{0:T(1024)S(1)} %get-tuple-element.112, f32[768]{0:T(1024)S(1)} %get-tuple-element.40, ...), kind=kOutput, calls=%fused_computation.361 | convolution fusion | flops 7256013312 | bytes 23627776 | tf_op jit(solution)/shard_map/dot_general | solution.py:66
  212.3 0.6 multiply_reduce_fusion.2
  213.6 1.1 add_convert_fusion.1
  214.7 8.8 %fusion.134 = f32[1536,2304]{1,0:T(8,128)S(1)} fusion(bf16[1536,768]{1,0:T(8,128)(2,1)S(1)} %add_convert_fusion.1, bf16[2,768,2304]{2,1,0:T(8,128)(2,1)} %param.27), kind=kOutput, calls=%fused_computation.165 | convolution fusion | flops 5435817984 | bytes 20054016 | tf_op jit(solution)/shard_map/dot_general | solution.py:42
  223.5 5.0 copy-done.5
  228.5 1.6 slice.358
  230.2 8.2 %reshape.284 = bf16[3,512,12,64]{3,2,1,0:T(8,128)(2,1)} reshape(bf16[1536,768]{1,0:T(8,128)(2,1)} %slice.358) | data formatting | bytes 4718592 | tf_op jit(solution)/shard_map/reshape | solution.py:44
  238.4 6.7 fusion.97
  245.1 8.2 reshape.283
  253.3 21.2 %fusion.103 = f32[3,12,512,512]{2,3,1,0:T(8,128)} fusion(bf16[3,512,12,64]{3,2,1,0:T(8,128)(2,1)} %reshape.284, bf16[3,512,12,64]{3,2,1,0:T(8,128)(2,1)} %reshape.283), kind=kOutput, calls=%fused_computation.137 | convolution fusion | flops 1207959552 | bytes 42467328 | tf_op jit(solution)/shard_map/gqhd,gkhd->ghqk/dot_general | solution.py:48
  274.5 39.8 %fusion.296 = (f32[3,12,512]{2,1,0:T(8,128)S(1)}, f32[3,12,512,512]{2,3,1,0:T(8,128)}) fusion(f32[3,12,512,512]{2,3,1,0:T(8,128)} %fusion.103, pred[3,512]{1,0:T(4,128)(4,1)S(1)} %copy-done.31), kind=kOutput, calls=%fused_computation.362 | output fusion | flops 56623616 | bytes 75572736 | tf_op jit(solution)/shard_map/sub | solution.py:54
  314.3 8.2 %reshape.282 = bf16[3,512,12,64]{3,2,1,0:T(8,128)(2,1)} reshape(bf16[1536,768]{1,0:T(8,128)(2,1)} %get-tuple-element.67) | data formatting | bytes 4718592 | tf_op jit(solution)/shard_map/reshape | solution.py:46
  322.5 16.1 %convert_bitcast_fusion = bf16[3,512,12,64]{1,3,2,0:T(8,128)(2,1)S(1)} fusion(f32[3,12,512,512]{2,3,1,0:T(8,128)} %get-tuple-element.97, f32[3,12,512]{2,1,0:T(8,128)S(1)} %get-tuple-element.96, bf16[3,512,12,64]{3,2,1,0:T(8,128)(2,1)} %reshape.282), kind=kOutput, calls=%fused_computation.186 | convolution fusion | flops 1228013568 | bytes 42541056 | tf_op jit(solution)/shard_map/ghqk,gkhd->gqhd/dot_general | solution.py:56
  338.6 2.0 copy.81
  340.6 0.8 copy.113
  341.6 2.4 fusion.297
  343.9 0.6 multiply_reduce_fusion.1
  344.7 50.0 %fusion.9.clone.3.clone.5 = bf16[1536,3072]{1,0:T(8,128)(2,1)} fusion(f32[3072]{0:T(1024)S(1)} %bitcast.186, bf16[2,768,3072]{2,1,0:T(8,128)(2,1)S(1)} %bitcast.191, f32[1536,768]{1,0:T(8,128)S(1)} %get-tuple-element.99, f32[768]{0:T(1024)S(1)} %copy-done.28, f32[768]{0:T(1024)S(1)} %copy-done.26, ...), kind=kOutput, calls=%fused_computation.20.clone.clone.clone.clone.clone.clone.clone.2 | convolution fusion | flops 7565082624 | bytes 18911232 | tf_op jit(solution)/shard_map/dot_general | solution.py:63
  394.7 12.2 %fusion.298 = (f32[1536]{0:T(1024)S(1)}, f32[1536,768]{1,0:T(8,128)S(1)}) fusion(f32[768]{0:T(1024)S(1)} %copy-done.27, bf16[2,3072,768]{2,1,0:T(8,128)(2,1)} %param.36, f32[1536,768]{1,0:T(8,128)S(1)} %get-tuple-element.99, f32[768]{0:T(1024)S(1)} %copy-done.28, f32[768]{0:T(1024)S(1)} %copy-done.26, f32[1536]{0:T(1024)S(1)} %add_rsqrt_fusion.1, ...), kind=kOutput, calls=%fused_computation.364 | convolution fusion | flops 7256013312 | bytes 23620608 | tf_op jit(solution)/shard_map/dot_general | solution.py:66
  407.8 1.1 add_convert_fusion
  409.0 0.9 fusion.185
  409.9 0.9 fusion.179
  411.6 0.8 fusion.307
  412.7 0.8 fusion.308
  413.5 2.5 fusion.208
  416.0 3.2 reshape.241
  419.5 2.5 fusion.209
  422.0 3.2 reshape.243
  426.1 46.9 %concatenate.3 = f32[1185801]{0:T(1024)} concatenate(f32[589824]{0:T(1024)} %reshape.241, f32[768]{0:T(1024)S(1)} %get-tuple-element.106, f32[2304]{0:T(1024)S(1)} %reshape.242, f32[3]{0:T(128)S(1)} %get-tuple-element.86, f32[589824]{0:T(1024)} %reshape.243, f32[768]{0:T(1024)S(1)} %get-tuple-element.108, f32[2304]{0:T(1024)S(1)} %reshape.244, f32[3]{0:T(128)S(1)} %get-tuple-element.60, ...), dimensions={0} | concatenate | bytes 9486408 | tf_op jit(solution)/shard_map/concatenate | solution.py:172
  473.0 4.2 pad.4
  477.2 147.8 %all-reduce.8.cloned.1.call-done = f32[1185824]{0:T(1024)} async-done(((f32[1185824]{0:T(1024)}), f32[1185824]{0:T(1024)}) %all-reduce.8.cloned.1.call-update) | async-done | bytes 4743312
  625.0 2.5 broadcast.332
  627.6 1.8 dynamic-slice_dynamic-update-slice_fusion
  630.2 4.3 pad_maximum_fusion
  634.5 140.5 %all-reduce.6.cloned.1.call-done = f32[1185824]{0:T(1024)} async-done(((f32[1185824]{0:T(1024)}), f32[1185824]{0:T(1024)}) %all-reduce.6.cloned.1.call-update) | async-done | bytes 4743312
  775.0 1.4 fusion.286
  776.4 4.3 fusion.197
  780.7 4.3 fusion.191
  787.7 5.2 slice_divide_fusion.1
  792.8 1.7 div.174
  794.5 3.5 div.172
  798.0 1.4 slice_divide_fusion.5
  799.4 1.4 slice_divide_fusion.3
  803.0 4.9 pad_maximum_fusion.1
  809.1 1.4 fusion.215
  (142 shorter events, 13.1 us)
Async XLA Ops:
  7.2 2.2 copy-start
  7.2 617.8 %all-reduce.8.cloned.1.call-start = ((), (), s32[]{:S(2)}) async-start(), calls=%async_computation.1 | async-start | bytes 9494528
  23.9 5.1 copy-start.4
  29.0 6.8 copy-start.17
  29.0 6.8 copy-start.18
  43.2 8.2 %copy-start.2 = (s32[3]{0:T(128)S(1)}, s32[3]{0:T(128)}, u32[]{:S(2)}) copy-start(s32[3]{0:T(128)} %param.24) | copy-start | bytes 40
  52.1 29.2 %copy-start.30 = (pred[3,512]{1,0:T(4,128)(4,1)}, pred[3,512]{1,0:T(4,128)(4,1)S(1)}, u32[]{:S(2)}) copy-start(pred[3,512]{1,0:T(4,128)(4,1)S(1)} %iota_compare_fusion) | copy-start | bytes 4612
  137.4 4.4 copy-start.3
  139.4 2.7 copy-start.19
  142.8 5.2 copy-start.9
  142.8 5.8 copy-start.20
  142.8 5.8 copy-start.21
  142.8 58.7 %slice-start.5 = ((s8[9437184]{0:T(1024)(128)(4,1)}), s8[4194304]{0:T(1024)(128)(4,1)S(1)}, s32[]{:S(2)}) async-start(s8[9437184]{0:T(1024)(128)(4,1)} %bitcast.192), calls=%async_computation.7 | async-start | bytes 8388608
  149.2 52.3 %slice-start.6 = ((s8[9437184]{0:T(1024)(128)(4,1)}), s8[4194304]{0:T(1024)(128)(4,1)S(1)}, s32[]{:S(2)}) async-start(s8[9437184]{0:T(1024)(128)(4,1)} %bitcast.192), calls=%async_computation.8 | async-start | bytes 8388608
  149.2 52.3 %slice-start.7 = ((s8[9437184]{0:T(1024)(128)(4,1)}), s8[1048576]{0:T(1024)(128)(4,1)S(1)}, s32[]{:S(2)}) async-start(s8[9437184]{0:T(1024)(128)(4,1)} %bitcast.192), calls=%async_computation.9 | async-start | bytes 2097152
  201.6 11.4 %copy-start.22 = (f32[2,768]{1,0:T(2,128)S(1)}, f32[2,768]{1,0:T(2,128)}, u32[]{:S(2)}) copy-start(f32[2,768]{1,0:T(2,128)} %param.39) | copy-start | bytes 18436
  201.6 11.4 %copy-start.23 = (f32[2,768]{1,0:T(2,128)S(1)}, f32[2,768]{1,0:T(2,128)}, u32[]{:S(2)}) copy-start(f32[2,768]{1,0:T(2,128)} %param.38) | copy-start | bytes 18436
  214.6 126.8 %copy-start.6 = (bf16[1536,768]{1,0:T(8,128)(2,1)}, bf16[1536,768]{1,0:T(8,128)(2,1)S(1)}, u32[]{:S(2)}) copy-start(bf16[1536,768]{1,0:T(8,128)(2,1)S(1)} %add_convert_fusion.1) | copy-start | bytes 7077892
  223.5 5.1 copy-start.5
  228.5 9.9 %copy-start.11 = (f32[768]{0:T(1024)S(1)}, f32[768]{0:T(1024)}, u32[]{:S(2)}) copy-start(f32[768]{0:T(1024)} %get-tuple-element.49) | copy-start | bytes 9220
  228.5 9.9 %copy-start.12 = (f32[768]{0:T(1024)S(1)}, f32[768]{0:T(1024)}, u32[]{:S(2)}) copy-start(f32[768]{0:T(1024)} %get-tuple-element.111) | copy-start | bytes 9220
  253.3 21.2 %copy-start.31 = (pred[3,512]{1,0:T(4,128)(4,1)S(1)}, pred[3,512]{1,0:T(4,128)(4,1)}, u32[]{:S(2)}) copy-start(pred[3,512]{1,0:T(4,128)(4,1)} %copy-done.30) | copy-start | bytes 4612
  338.6 2.9 copy-start.25
  338.6 2.9 copy-start.33
  340.6 3.9 slice-start.2
  341.5 3.1 copy-start.15
  341.5 3.1 copy-start.26
  341.5 3.1 copy-start.28
  341.5 3.1 slice-start.3
  341.5 3.1 slice-start.4
  344.6 50.0 %copy-start.27 = (f32[768]{0:T(1024)S(1)}, f32[768]{0:T(1024)}, u32[]{:S(2)}) copy-start(f32[768]{0:T(1024)} %get-tuple-element.43) | copy-start | bytes 9220
  394.7 14.3 %slice-start = ((s8[4718592]{0:T(1024)(128)(4,1)}), s8[4194304]{0:T(1024)(128)(4,1)S(1)}, s32[]{:S(2)}) async-start(s8[4718592]{0:T(1024)(128)(4,1)} %bitcast.175), calls=%async_computation.2 | async-start | bytes 8388608
  394.7 13.0 %copy-start.32 = (f32[2,3]{1,0:T(2,128)S(1)}, f32[2,3]{1,0:T(2,128)}, u32[]{:S(2)}) copy-start(f32[2,3]{1,0:T(2,128)} %param.43) | copy-start | bytes 76
  394.7 13.0 %copy-start.24 = (f32[2,768]{1,0:T(2,128)S(1)}, f32[2,768]{1,0:T(2,128)}, u32[]{:S(2)}) copy-start(f32[2,768]{1,0:T(2,128)} %param.41) | copy-start | bytes 18436
  394.7 13.0 %copy-start.13 = (f32[768]{0:T(1024)S(1)}, f32[768]{0:T(1024)}, u32[]{:S(2)}) copy-start(f32[768]{0:T(1024)} %get-tuple-element.37) | copy-start | bytes 9220
  394.7 13.0 %copy-start.14 = (f32[768]{0:T(1024)S(1)}, f32[768]{0:T(1024)}, u32[]{:S(2)}) copy-start(f32[768]{0:T(1024)} %get-tuple-element.115) | copy-start | bytes 9220
  394.7 14.3 %slice-start.1 = ((s8[4718592]{0:T(1024)(128)(4,1)}), s8[524288]{0:T(1024)(128)(4,1)S(1)}, s32[]{:S(2)}) async-start(s8[4718592]{0:T(1024)(128)(4,1)} %bitcast.175), calls=%async_computation.3 | async-start | bytes 1048576
  407.0 1.9 copy-start.10
  407.0 2.0 copy-start.7
  407.7 3.5 copy-start.16
  407.7 3.5 copy-start.29
  408.9 1.9 copy-start.8
  477.2 297.8 %all-reduce.6.cloned.1.call-start = ((), (), s32[]{:S(2)}) async-start(), calls=%async_computation | async-start | bytes 9494528
  794.5 16.5 %copy-start.1 = (bf16[3,512,768]{2,1,0:T(8,128)(2,1)S(1)}, bf16[3,512,768]{2,1,0:T(8,128)(2,1)}, u32[]{:S(2)}) copy-start(bf16[3,512,768]{2,1,0:T(8,128)(2,1)} %param.23) | copy-start | bytes 7077892
Sparse Core Ops, SparseCore 0:
  477.3 147.6 all-reduce.7
  630.8 144.1 all-reduce.5
where the time goes:
time: 827 us; the launch traced here: 818 us
  waiting for transfers between devices  288 us (35%)
  matrix products  241 us (29%)
  local copies, waits for them, and re-layouts  147 us (18%)
  other arithmetic  124 us (15%)
  between operations  17.7 us (2%)
    unnamed x4, waiting for transfers between devices  288 us
    dot_general x2, matrix products, block_forward(): jnp.dot(middle.astype(bf16), w_in, preferred_element_type=f32) + b_in  102 us
    sub x2, other arithmetic, block_forward(): raised = jnp.exp(scores - highest)  79.6 us
    concatenate x1, local copies, waits for them, and re-layouts, local(): bucket = jnp.concatenate(pieces)  46.9 us
    dot_general x2, matrix products, block_forward(): jnp.einsum('gqhd,gkhd->ghqk', queries, keys_low, preferred_element_type=f32)  42.2 us
    dot_general x2, matrix products, block_forward(): jnp.einsum('ghqk,gkhd->gqhd', probs, values_low, preferred_element_type=f32)  32.4 us
    dot_general x2, matrix products, block_forward(): jnp.dot(expanded, w_back, preferred_element_type=f32)  22.9 us
    unnamed x90, local copies, waits for them, and re-layouts  18.9 us
  transfers between devices with their start and end apart: 2, of which 2 were waited for; matrix products, arithmetic and copies ran while one was open for 1% of the time, Pallas kernels for 0%

commit v1 on v0

v1 whole, which is shorter than its diff:
```python
import functools
import math

import jax
import jax.numpy as jnp
from jax import lax
from jax.experimental import pallas as pl
from jax.experimental.pallas import tpu as pltpu
from jax.sharding import PartitionSpec as P

HEAD = 64
PRECISE = lax.Precision.HIGHEST
epsilon = 1e-12
bf16 = jnp.bfloat16
f32 = jnp.float32
SCALE = HEAD**-0.5 * math.log2(math.e)
SUM_LOW = 2.0**-60
SUM_HIGH = 2.0**100


def gelu(values):
    return (0.5 * values) * (1.0 + lax.erf(values * math.sqrt(0.5)))


def norm_rows(values, gain, shift):
    center = values - jnp.mean(values, -1, keepdims=True)
    spread = jnp.mean(center * center, -1, keepdims=True)
    return center * lax.rsqrt(spread + epsilon) * gain + shift


def blocks_kernel(
    order,
    lens,
    hidden,
    w_qkv,
    w_out,
    w_in,
    w_back,
    b_query,
    b_value,
    b_out,
    ln1_gain,
    ln1_bias,
    b_in,
    b_back,
    ln2_gain,
    ln2_bias,
    states,
    firsts,
    x_buf,
    qkv_buf,
    out_buf,
    in_buf,
    back_buf,
    turned,
    columns,
    q_buf,
    k_buf,
    v_buf,
    p_buf,
    ct_buf,
    c_buf,
    m_buf,
    mb_buf,
    h_buf,
    fine,
    vec_buf,
    unit_buf,
    w_sem,
    x_sem,
    o_sem,
):
    depth, width = b_query.shape
    slots, length = x_buf.shape[1], x_buf.shape[2]
    heads = width // HEAD
    hidden_units = b_in.shape[1]

    def fetch_x(s):
        return pltpu.make_async_copy(hidden.at[order[s]], x_buf.at[0, s], x_sem.at[s])

    def fetch_qkv(l, part):
        cols = pl.ds(pl.multiple_of(part * width, 128), width)
        return pltpu.make_async_copy(
            w_qkv.at[l, :, cols], qkv_buf.at[l, :, cols], w_sem.at[l, part]
        )

    def fetch_rest(l, number):
        source = (w_out, w_in, w_back)[number]
        target = (out_buf, in_buf, back_buf)[number]
        return pltpu.make_async_copy(source.at[l], target.at[l], w_sem.at[l, 3 + number])

    def put_states(l, s):
        return pltpu.make_async_copy(x_buf.at[l + 1, s], states.at[l, s], o_sem.at[l, s])

    fetch_qkv(0, 0).start()
    fetch_qkv(0, 2).start()
    fetch_x(0).start()
    fetch_qkv(0, 1).start()
    for s in range(1, slots):
        fetch_x(s).start()
    for number in range(3):
        fetch_rest(0, number).start()
    for l in range(1, depth):
        for part in range(3):
            fetch_qkv(l, part).start()
        for number in range(3):
            fetch_rest(l, number).start()

    q_buf[...] = jnp.zeros_like(q_buf)
    vectors = (b_query, b_value, b_out, ln1_gain, ln1_bias, b_back, ln2_gain, ln2_bias)
    for l in range(depth):
        for number, vector in enumerate(vectors):
            vec_buf[l, number : number + 1] = vector[l : l + 1]
        unit_buf[l, 0:1] = b_in[l : l + 1]

    def project(l, s):
        rows = x_buf[l, s]
        k_buf[...] = jnp.dot(
            rows, qkv_buf[l, :, width : 2 * width], preferred_element_type=f32
        ).astype(bf16)
        count = lens[order[s]]
        seen = (
            lax.broadcasted_iota(jnp.int32, (HEAD, length), 1) < count
        ).astype(f32)
        joined = lax.dot_general(
            turned[...], rows, (((1,), (1,)), ((), ())), preferred_element_type=f32
        )
        for h in range(heads):
            at = slice(h * HEAD, (h + 1) * HEAD)
            half = slice((h % 2) * HEAD, (h % 2 + 1) * HEAD)
            q_buf[h, half] = (
                joined[at] + jnp.tile(columns[at, :], (1, length // 128))
            ).astype(bf16)
            av = slice(width + h * HEAD, width + (h + 1) * HEAD)
            v_buf[h, :HEAD] = (
                (joined[av] + jnp.tile(columns[av, :], (1, length // 128))) * seen
            ).astype(bf16)
            v_buf[h, HEAD:] = seen.astype(bf16)

    def attend(s):
        def score(h):
            pair = slice((h // 2) * 128, (h // 2 + 1) * 128)
            scores = jnp.dot(k_buf[:, pair], q_buf[h], preferred_element_type=f32)
            p_buf[h % 4] = jnp.exp2(scores * SCALE).astype(bf16)

        def mix(h):
            both = jnp.dot(v_buf[h], p_buf[h % 4], preferred_element_type=f32)
            sums = both[HEAD:]
            good = (sums[:8] >= SUM_LOW) & (sums[:8] <= SUM_HIGH)
            fine[...] = jnp.where(good, fine[...], 0.0)
            half = slice((h % 2) * HEAD, (h % 2 + 1) * HEAD)
            ct_buf[(h // 2) % 2, half] = (both[:HEAD] * (1.0 / sums)).astype(bf16)
            if h % 2 == 1:
                pair = slice((h // 2) * 128, (h // 2 + 1) * 128)
                c_buf[s, :, pair] = ct_buf[(h // 2) % 2].T

        score(0)
        for h in range(heads):
            if h + 1 < heads:
                score(h + 1)
            mix(h)

    def attend_shifted(s):
        count = lens[order[s]]

        def pair_step(number, carry):
            lanes = pl.ds(pl.multiple_of(number * 128, 128), 128)
            for side in range(2):
                h = number * 2 + side
                scores = (
                    jnp.dot(k_buf[:, lanes], q_buf[h], preferred_element_type=f32) * SCALE
                )
                seen = lax.broadcasted_iota(jnp.int32, scores.shape, 0) < count
                scores = jnp.where(seen, scores, -1e30)
                highest = jnp.max(scores, 0, keepdims=True)
                p_buf[side] = jnp.exp2(scores - highest).astype(bf16)
                both = jnp.dot(v_buf[h], p_buf[side], preferred_element_type=f32)
                ct_buf[0, side * HEAD : (side + 1) * HEAD] = (
                    both[:HEAD] / both[HEAD:]
                ).astype(bf16)
            c_buf[s, :, lanes] = ct_buf[0].T
            return carry

        lax.fori_loop(0, heads // 2, pair_step, 0)

    def feed(l, s):
        tile = length // 2
        spans = [slice(t * tile, (t + 1) * tile) for t in range(2)]
        shift_out, gain1, shift1, shift_back, gain2, shift2 = (
            vec_buf[l, number : number + 1] for number in range(2, 8)
        )
        for span in spans:
            attended = jnp.dot(c_buf[s, span], out_buf[l], preferred_element_type=f32)
            values = x_buf[l, s, span].astype(f32) + (attended + shift_out)
            middle = norm_rows(values, gain1, shift1)
            m_buf[span] = middle
            mb_buf[span] = middle.astype(bf16)
        chunk = 512
        for span in spans:
            for j in range(hidden_units // chunk):
                units = slice(j * chunk, (j + 1) * chunk)
                inner = jnp.dot(
                    mb_buf[span], in_buf[l, :, units], preferred_element_type=f32
                )
                h_buf[span, units] = gelu(inner + unit_buf[l, 0:1, units]).astype(bf16)
        for span in spans:
            back = jnp.dot(h_buf[span], back_buf[l], preferred_element_type=f32)
            values = m_buf[span] + back + shift_back
            x_buf[l + 1, s, span] = norm_rows(
                values, gain2, shift2
            ).astype(bf16)

    def layer(l, carry):
        for part in range(3):
            fetch_qkv(l, part).wait()
        for part, offset in ((0, 0), (2, width)):
            for j in range(width // 128):
                cols = slice(part * width + j * 128, part * width + (j + 1) * 128)
                turned[offset + j * 128 : offset + (j + 1) * 128] = qkv_buf[l, :, cols].T
        for j in range(width // 128):
            lanes = slice(j * 128, (j + 1) * 128)
            for number in range(2):
                offset = number * width + j * 128
                columns[offset : offset + 128] = jnp.broadcast_to(
                    vec_buf[l, number : number + 1, lanes], (128, 128)
                ).T
        fine[...] = jnp.ones_like(fine)

        def front(s, carry):
            @pl.when(l == 0)
            def _():
                fetch_x(s).wait()

            project(l, s)
            attend(s)
            return carry

        lax.fori_loop(0, slots, front, 0)

        @pl.when(jnp.min(fine[...]) < 0.5)
        def _():
            def again(s, carry):
                project(l, s)
                attend_shifted(s)
                return carry

            lax.fori_loop(0, slots, again, 0)

        for number in range(3):
            fetch_rest(l, number).wait()

        def rear(s, carry):
            feed(l, s)
            put_states(l, s).start()
            return carry

        lax.fori_loop(0, slots, rear, 0)
        return carry

    lax.fori_loop(0, depth, layer, 0)
    for l in range(depth):
        for s in range(slots):
            number = l * slots + s
            firsts[number : number + 1] = x_buf[l + 1, s, 0:1].astype(f32)
            put_states(l, s).wait()


def run_blocks(hidden, lengths, slot_order, stacks):
    (
        w_qkv,
        b_query,
        b_value,
        w_out,
        b_out,
        ln1_gain,
        ln1_bias,
        w_in,
        b_in,
        w_back,
        b_back,
        ln2_gain,
        ln2_bias,
    ) = stacks
    slots, length, width = hidden.shape
    depth = w_qkv.shape[0]
    units = w_in.shape[2]
    heads = width // HEAD
    place_hbm = pl.BlockSpec(memory_space=pl.ANY)
    place_smem = pl.BlockSpec(memory_space=pltpu.SMEM)
    place_vmem = pl.BlockSpec(memory_space=pltpu.VMEM)
    return pl.pallas_call(
        blocks_kernel,
        name="blocks",
        out_shape=(
            jax.ShapeDtypeStruct((depth, slots, length, width), bf16),
            jax.ShapeDtypeStruct((depth * slots, width), f32),
        ),
        in_specs=[place_smem] * 2 + [place_hbm] * 5 + [place_vmem] * 9,
        out_specs=(place_hbm, place_vmem),
        scratch_shapes=[
            pltpu.VMEM((depth + 1, slots, length, width), bf16),
            pltpu.VMEM((depth, width, 3 * width), bf16),
            pltpu.VMEM((depth, width, width), bf16),
            pltpu.VMEM((depth, width, units), bf16),
            pltpu.VMEM((depth, units, width), bf16),
            pltpu.VMEM((2 * width, width), bf16),
            pltpu.VMEM((2 * width, 128), f32),
            pltpu.VMEM((heads, 2 * HEAD, length), bf16),
            pltpu.VMEM((length, width), bf16),
            pltpu.VMEM((heads, 2 * HEAD, length), bf16),
            pltpu.VMEM((4, length, length), bf16),
            pltpu.VMEM((2, 2 * HEAD, length), bf16),
            pltpu.VMEM((slots, length, width), bf16),
            pltpu.VMEM((length, width), f32),
            pltpu.VMEM((length, width), bf16),
            pltpu.VMEM((length, units), bf16),
            pltpu.VMEM((8, length), f32),
            pltpu.VMEM((depth, 8, width), f32),
            pltpu.VMEM((depth, 8, units), f32),
            pltpu.SemaphoreType.DMA((depth, 6)),
            pltpu.SemaphoreType.DMA((slots,)),
            pltpu.SemaphoreType.DMA((depth, slots)),
        ],
        compiler_params=pltpu.CompilerParams(vmem_limit_bytes=62 * 1024 * 1024),
    )(
        slot_order,
        lengths,
        hidden,
        w_qkv,
        w_out,
        w_in,
        w_back,
        b_query,
        b_value,
        b_out,
        ln1_gain,
        ln1_bias,
        b_in,
        b_back,
        ln2_gain,
        ln2_bias,
    )


def ramp(firsts, labels, count, own, own_labels, pool_w, pool_b, cls_w, cls_b):
    classes = jnp.arange(cls_w.shape[1], dtype=jnp.int32)[None, :]

    def forward(states):
        pooled = jnp.tanh(jnp.dot(states, pool_w, precision=PRECISE) + pool_b)
        return pooled, jnp.dot(pooled, cls_w, precision=PRECISE) + cls_b

    def backward(pooled, scores, label_values):
        highest = jnp.max(scores, -1, keepdims=True)
        raised = jnp.exp(scores - highest)
        totals = jnp.sum(raised, -1, keepdims=True)
        onehot = (label_values[:, None] == classes).astype(f32)
        labelled = (label_values >= 0).astype(f32)
        log_total = highest[:, 0] + jnp.log(totals[:, 0])
        loss = jnp.sum(labelled * (log_total - jnp.sum(scores * onehot, -1))) / count
        grad = labelled[:, None] * (raised / totals - onehot) / count
        inner = jnp.dot(grad, cls_w.T, precision=PRECISE) * (1.0 - pooled * pooled)
        return loss, grad, inner

    pooled, scores = forward(firsts)
    loss, grad, inner = backward(pooled, scores, labels)
    own_pooled, own_scores = forward(own)
    _, _, own_inner = backward(own_pooled, own_scores, own_labels)
    return (
        own_scores,
        loss,
        jnp.dot(firsts.T, inner, precision=PRECISE),
        jnp.sum(inner, 0),
        jnp.dot(pooled.T, grad, precision=PRECISE),
        jnp.sum(grad, 0),
        jnp.dot(own_inner, pool_w.T, precision=PRECISE),
    )


def local(
    hidden,
    lengths,
    slot_order,
    labels,
    w_qkv,
    b_query,
    b_value,
    w_out,
    b_out,
    ln1_gain,
    ln1_bias,
    w_in,
    b_in,
    w_back,
    b_back,
    ln2_gain,
    ln2_bias,
    pool_w,
    pool_b,
    cls_w,
    cls_b,
):
    depth = w_qkv.shape[0]
    slots, _, width = hidden.shape
    stacks = (
        w_qkv,
        b_query,
        b_value,
        w_out,
        b_out,
        ln1_gain,
        ln1_bias,
        w_in,
        b_in,
        w_back,
        b_back,
        ln2_gain,
        ln2_bias,
    )
    states, firsts = run_blocks(hidden, lengths, slot_order, stacks)
    own_labels = jnp.take(labels, slot_order, axis=0)
    marks = jnp.zeros((8 - depth * slots % 8, width), f32)
    marks = marks.at[0, :slots].set(own_labels.astype(f32))
    packet = jnp.concatenate([firsts, marks])
    gathered = lax.all_gather(packet, "narrow", axis=0, tiled=False)
    gathered = lax.all_gather(gathered, "wide", axis=0, tiled=False)
    gathered = gathered.reshape(-1, packet.shape[0], width)
    all_labels = gathered[:, depth * slots, :slots].reshape(-1).astype(jnp.int32)
    count = jnp.sum((all_labels >= 0).astype(f32))
    results = []
    for l in range(depth):
        mine = slice(l * slots, (l + 1) * slots)
        results.append(
            ramp(
                gathered[:, mine].reshape(-1, width),
                all_labels,
                count,
                firsts[mine],
                own_labels,
                pool_w[l],
                pool_b[l],
                cls_w[l],
                cls_b[l],
            )
        )
    return (states,) + tuple(jnp.stack(members) for members in zip(*results))


def solution(mesh):
    both = ("wide", "narrow")
    return jax.shard_map(
        local,
        mesh=mesh,
        in_specs=(P(both, None, None), P(both), P(both), P(both)) + (P(),) * 17,
        out_specs=(
            P(None, both, None, None),
            P(None, both, None),
            P(),
            P(),
            P(),
            P(),
            P(),
            P(None, both, None),
        ),
        check_vma=False,
    )
```

time: 827 us -> 147 us (0.18); the launches traced: 818 us -> 147 us
  waiting for transfers between devices: 288 us -> 0 us
  matrix products: 241 us -> 28 us
  local copies, waits for them, and re-layouts: 147 us -> 5.77 us
  other arithmetic: 124 us -> 7.16 us
  Pallas kernels: 0 us -> 77 us
  blocking collectives: 0 us -> 25.4 us
  between operations: 17.7 us -> 3.58 us
    unnamed x4 -> x0, waiting for transfers between devices: 288 us -> none
    dot_general x24 -> x18, matrix products: 241 us -> 28 us  [the longest x4 12.1 us: forward(): pooled = jnp.tanh(jnp.dot(states, pool_w, precision=PRECISE) + pool_b)]
    sub x2 -> x1, other arithmetic: 79.6 us -> 0.01 us  [backward(): log_total - jnp.sum(scores * onehot, -1)]
    pallas_call x0 -> x1, Pallas kernels: none -> 77 us  [run_blocks(): pl.pallas_call(blocks_kernel, name='blocks', out_shape=(jax.ShapeDtypeStr...]
    reshape x10 -> x2, local copies, waits for them, and re-layouts: 54.5 us -> 0.3 us  [local(): gathered[:, mine].reshape(-1, width)]
    concatenate x1 -> x0, local copies, waits for them, and re-layouts: 46.9 us -> none  [local(): bucket = jnp.concatenate(pieces)]
    all_gather x0 -> x2, blocking collectives: none -> 25.4 us  [the longest x1 15 us: local(): gathered = lax.all_gather(packet, 'narrow', axis=0, tiled=False)]
    unnamed x90 -> x7, local copies, waits for them, and re-layouts: 18.9 us -> 1.84 us
  transfers between devices with their start and end apart: 2 -> 0, of which waited for: 2 -> 0; matrix products, arithmetic and copies ran while one was open for 1% -> 0% of each run, Pallas kernels for 0% -> 0%
where the time goes in v1:
time: 147 us
  Pallas kernels  77 us (52%)
  matrix products  28 us (19%)
  blocking collectives  25.4 us (17%)
  other arithmetic  7.16 us (5%)
  local copies, waits for them, and re-layouts  5.77 us (4%)
  between operations  3.58 us (2%)
    pallas_call x1, Pallas kernels, run_blocks(): pl.pallas_call(blocks_kernel, name='blocks', out_shape=(jax.ShapeDtypeStr...  77 us
    all_gather x1, blocking collectives, local(): gathered = lax.all_gather(packet, 'narrow', axis=0, tiled=False)  15 us
    dot_general x4, matrix products, forward(): pooled = jnp.tanh(jnp.dot(states, pool_w, precision=PRECISE) + pool_b)  12.1 us
    all_gather x1, blocking collectives, local(): gathered = lax.all_gather(gathered, 'wide', axis=0, tiled=False)  10.4 us
    dot_general x2, matrix products, ramp(): jnp.dot(own_inner, pool_w.T, precision=PRECISE)  7.31 us
    another operation x7, other arithmetic, local(): return (states,) + tuple((jnp.stack(members) for members in zip(*results)))  4.29 us
    dot_general x2, matrix products, ramp(): jnp.dot(firsts.T, inner, precision=PRECISE)  4.25 us

profile of v1, /device:TPU:0, one launch (start us, length us, event | category | flops | bytes accessed | tf_op | source)
XLA Modules:
  0.0 146.9 jit_solution(17990433858265766092)
XLA Ops:
  0.6 0.0 copy-start
  0.6 0.7 compare_select_fusion
  1.3 0.8 slice_bitcast_fusion.1
  2.1 0.0 copy-done
  2.1 0.6 gather_fusion
  2.7 0.7 compare_convert_fusion
  3.4 0.8 slice_reduce_fusion.1
  4.2 0.8 fusion.87
  5.0 77.0 %blocks.1 = (bf16[2,3,512,768]{3,2,1,0:T(8,128)(2,1)}, f32[6,768]{1,0:T(8,128)}) custom-call(s32[3]{0:T(128)} %order.1, s32[3]{0:T(128)} %lens.1, bf16[3,512,768]{2,1,0:T(8,128)(2,1)} %hidden.1, bf16[2,768,2304]{2,1,0:T(8,128)(2,1)} %w_qkv.1, bf16[2,768,768]{2,1,0:T(8,128)(2,1)} %w_out.1, bf16[2,768,3072]{2,1,0:T(8,128)(2,1)} %w_in.1, ...), custom_call_target="tpu_custom_call" | custom-call | tf_op jit(solution)/shard_map/blocks/pallas_call | solution.py:291
  82.0 0.0 copy-start.1
  82.0 2.9 %fusion.42 = f32[3,768]{1,0:T(4,128)S(1)} fusion(f32[2,768,768]{2,1,0:T(8,128)} %param.40, f32[6,768]{1,0:T(8,128)} %get-tuple-element.23, f32[768]{0:T(1024)S(1)} %get-tuple-element.49), kind=kOutput, calls=%fused_computation.36 | convolution fusion | flops 21235968 | bytes 2383872 | tf_op jit(solution)/shard_map/dot_general | solution.py:349
  84.9 0.2 fusion.92
  85.1 0.1 copy.44
  85.2 2.9 %fusion.33 = f32[3,768]{1,0:T(4,128)S(1)} fusion(f32[2,768,768]{2,1,0:T(8,128)} %param.40, f32[6,768]{1,0:T(8,128)} %get-tuple-element.23, f32[768]{0:T(1024)S(1)} %get-tuple-element.48), kind=kOutput, calls=%fused_computation.33 | convolution fusion | flops 21235968 | bytes 2383872 | tf_op jit(solution)/shard_map/dot_general | solution.py:349
  88.1 0.0 copy-done.1
  88.1 0.2 fusion.93
  88.3 0.1 copy.43
  88.4 0.6 copy.46
  89.0 15.0 %all-gather = f32[32,768]{1,0:T(8,128)S(1)} all-gather(f32[8,768]{1,0:T(8,128)S(1)} %select_maximum_fusion), channel_id=2, replica_groups=mesh['wide'=8,'narrow'=4] {'narrow'}, dimensions={0}, use_global_device_ids=true | all-gather | bytes 122880 | tf_op jit(solution)/shard_map/all_gather | solution.py:424
  104.1 10.4 %all-gather.1 = f32[32,8,768]{2,1,0:T(8,128)S(1)} all-gather(f32[4,8,768]{2,1,0:T(8,128)S(1)} %bitcast.110), channel_id=3, replica_groups=mesh['wide'=8,'narrow'=4] {'wide'}, dimensions={0}, use_global_device_ids=true | all-gather | bytes 884736 | tf_op jit(solution)/shard_map/all_gather | solution.py:425
  114.5 0.1 fusion.86
  114.6 0.1 reshape.155
  114.8 0.1 convert_element_type.47
  114.9 3.2 %fusion.27 = f32[96,768]{1,0:T(8,128)S(1)} fusion(f32[96,768]{1,0:T(8,128)S(1)} %reshape.155, f32[2,768,768]{2,1,0:T(8,128)} %param.40, f32[768]{0:T(1024)S(1)} %get-tuple-element.49), kind=kOutput, calls=%fused_computation.25 | convolution fusion | flops 679550976 | bytes 2952192 | tf_op jit(solution)/shard_map/dot_general | solution.py:349
  118.1 0.4 fusion.88
  118.4 0.2 reshape.154
  118.6 3.2 %fusion.21 = f32[96,768]{1,0:T(8,128)S(1)} fusion(f32[96,768]{1,0:T(8,128)S(1)} %reshape.154, f32[2,768,768]{2,1,0:T(8,128)} %param.40, f32[768]{0:T(1024)S(1)} %get-tuple-element.48), kind=kOutput, calls=%fused_computation.23 | convolution fusion | flops 679550976 | bytes 2952192 | tf_op jit(solution)/shard_map/dot_general | solution.py:349
  121.8 0.4 fusion.89
  122.2 0.1 sub.89
  122.3 0.1 sub.85
  122.4 0.6 select_reduce_fusion.1
  125.7 0.9 convolution_multiply_fusion.2
  126.6 0.9 convolution_multiply_fusion.3
  127.5 0.8 fusion.84
  128.3 0.6 pad_maximum_fusion.6
  128.9 0.6 pad_maximum_fusion.5
  129.4 3.6 %fusion.36 = f32[1,3,768]{2,1,0:T(4,128)S(1)} fusion(f32[3,768]{1,0:T(4,128)S(1)} %convolution_multiply_fusion.3, f32[2,768,768]{2,1,0:T(8,128)} %param.40), kind=kOutput, calls=%fused_computation.34 | convolution fusion | flops 21233664 | bytes 2377728 | tf_op jit(solution)/shard_map/dot_general | solution.py:375
  133.1 3.7 %fusion.45 = f32[1,3,768]{2,1,0:T(4,128)S(1)} fusion(f32[3,768]{1,0:T(4,128)S(1)} %convolution_multiply_fusion.2, f32[2,768,768]{2,1,0:T(8,128)} %param.40), kind=kOutput, calls=%fused_computation.37 | convolution fusion | flops 21233664 | bytes 2377728 | tf_op jit(solution)/shard_map/dot_general | solution.py:375
  136.8 0.6 copy.48
  137.4 0.3 convolution_bitcast_fusion.3
  137.7 0.5 fusion.91
  138.1 0.3 convolution_bitcast_fusion.2
  138.4 0.5 fusion.90
  138.9 0.6 pad_maximum_fusion.3
  139.5 0.6 copy.47
  140.1 2.1 %convolution_bitcast_fusion = f32[1,768,768]{2,1,0:T(8,128)S(1)} fusion(f32[96,768]{1,0:T(8,128)S(1)} %reshape.155, f32[96,768]{1,0:T(8,128)S(1)} %get-tuple-element.78), kind=kOutput, calls=%fused_computation.20 | convolution fusion | flops 679477248 | bytes 2949120 | tf_op jit(solution)/shard_map/dot_general | solution.py:371
  142.3 2.1 %convolution_bitcast_fusion.1 = f32[1,768,768]{2,1,0:T(8,128)S(1)} fusion(f32[96,768]{1,0:T(8,128)S(1)} %reshape.154, f32[96,768]{1,0:T(8,128)S(1)} %get-tuple-element.80), kind=kOutput, calls=%fused_computation.21 | convolution fusion | flops 679477248 | bytes 2949120 | tf_op jit(solution)/shard_map/dot_general | solution.py:371
  144.4 2.5 %pad_maximum_fusion = f32[2,768,768]{2,1,0:T(8,128)} fusion(f32[1,768,768]{2,1,0:T(8,128)S(1)} %convolution_bitcast_fusion, f32[1,768,768]{2,1,0:T(8,128)S(1)} %convolution_bitcast_fusion.1), kind=kLoop, calls=%fused_computation.1 | loop fusion | flops 1179648 | bytes 9437184 | tf_op jit(solution)/shard_map/stack | solution.py:445
  (15 shorter events, 0.2 us)
Async XLA Ops:
  0.6 1.4 copy-start
  82.0 6.1 %copy-start.1 = (f32[6,768]{1,0:T(8,128)S(1)}, f32[6,768]{1,0:T(8,128)}, u32[]{:S(2)}) copy-start(f32[6,768]{1,0:T(8,128)} %get-tuple-element.23) | copy-start | bytes 55300
